TPU v7x, 128 devices: a whole 4x4x4 slice. The times are simulated.
128 devices in a mesh: fsdp: 16 (over y, z_hi, core), tp: 8 (over x, z_lo).
Axes of the slice: x: 4, y: 4, z: 4 (z_hi: 2, z_lo: 2; z = z_hi * 2 + z_lo), core: 2. Of those that a mesh axis runs over, the one named last changes fastest.
Arguments:
- tokens: bfloat16 [16384, 2048], P(('fsdp', 'tp')), may hold values from -6 to 6
- seq_lens: int32 [16, 8], P('fsdp'), may hold values from 0 to 1024, as said below
- ln1_gain: bfloat16 [2048], P('fsdp'), may hold values from 0.25 to 1.75
- ln1_bias: bfloat16 [2048], P('fsdp'), may hold values from -3 to 3
- w_qkv: bfloat16 [2048, 3, 2048], P('fsdp', None, 'tp'), may hold values from -0.125 to 0.125
- b_qkv: bfloat16 [3, 32, 64], P(None, 'tp', 'fsdp'), may hold values from -3 to 3
- w_out: bfloat16 [2048, 2048], P('tp', 'fsdp'), may hold values from -0.5 to 0.5
- ln2_gain: bfloat16 [2048], P('fsdp'), may hold values from 0.25 to 1.75
- ln2_bias: bfloat16 [2048], P('fsdp'), may hold values from -3 to 3
- w_gate: bfloat16 [2048, 5632], P('fsdp', 'tp'), may hold values from -0.125 to 0.125
- w_up: bfloat16 [2048, 5632], P('fsdp', 'tp'), may hold values from -0.125 to 0.125
- w_down: bfloat16 [5632, 2048], P('tp', 'fsdp'), may hold values from -0.078125 to 0.078125
- cotangent: bfloat16 [16384, 2048], P(('fsdp', 'tp')), may hold values from -6 to 6
Outputs:
- output: bfloat16 [16384, 2048], P(('fsdp', 'tp'))
- d_tokens: float32 [16384, 2048], P(('fsdp', 'tp'))
- d_ln1_gain: float32 [2048], P('fsdp')
- d_ln1_bias: float32 [2048], P('fsdp')
- d_w_qkv: float32 [2048, 3, 2048], P('fsdp', None, 'tp')
- d_b_qkv: float32 [3, 32, 64], P(None, 'tp', 'fsdp')
- d_w_out: float32 [2048, 2048], P('tp', 'fsdp')
- d_ln2_gain: float32 [2048], P('fsdp')
- d_ln2_bias: float32 [2048], P('fsdp')
- d_w_gate: float32 [2048, 5632], P('fsdp', 'tp')
- d_w_up: float32 [2048, 5632], P('fsdp', 'tp')
- d_w_down: float32 [5632, 2048], P('tp', 'fsdp')
Inputs may be any that keep to these rules, and one draw needn't show every extreme that they name: `seq_lens`: each row lists the lengths of the sequences packed in order into the 1024 slots of one index of fsdp and sums to 1024; a zero is an empty entry; in one row a single sequence fills all 1024 slots.
All inputs are finite; a program needn't handle non-finite values.
Results may differ from a plain program's by a relative error of at most 0.035.
Values may be sent and summed in bfloat16 or wider, within the bound.
A program may use at most 192 MiB of HBM per device.

v0:
```python
import math

import jax
import jax.numpy as jnp
from jax import lax
from jax.sharding import PartitionSpec as P

HEAD_DIM = 64
ROT = 16


norm_eps = 1e-05
rope_base = 10000.0
masked_value = -1e30


def layer_norm(values, gain_row, offset_row):
    center = values - jnp.mean(values, axis=-1, keepdims=True)
    spread = jnp.mean(center * center, axis=-1, keepdims=True)
    return center * lax.rsqrt(spread + norm_eps) * gain_row + offset_row


def slot_tables(lengths, total_rows):
    slot_ids = jnp.arange(total_rows, dtype=jnp.int32)
    seq_ends = jnp.cumsum(lengths, dtype=jnp.int32)
    before = (seq_ends[None, :] <= slot_ids[:, None]).astype(jnp.int32)
    segment = jnp.sum(before, axis=1, dtype=jnp.int32)
    seq_start = jnp.sum(before * lengths[None, :], axis=1, dtype=jnp.int32)
    return (segment, slot_ids - seq_start)


def rotate(values, position, rot_dims, direction):
    half_dims = rot_dims // 2
    frequency = jnp.exp(
        jnp.arange(half_dims, dtype=jnp.float32) * (-2.0 * math.log(rope_base) / rot_dims)
    )
    angles = position.astype(jnp.float32)[:, None] * frequency[None, :]
    cosine = jnp.cos(angles)[:, None, :]
    sine_part = direction * jnp.sin(angles)[:, None, :]
    first_half = values[..., :half_dims]
    second = values[..., half_dims:rot_dims]
    return jnp.concatenate(
        [
            first_half * cosine - second * sine_part,
            second * cosine + first_half * sine_part,
            values[..., rot_dims:],
        ],
        axis=-1,
    )


def local(
    tokens,
    seq_lens,
    ln1_gain,
    ln1_bias,
    w_qkv,
    b_qkv,
    w_out,
    ln2_gain,
    ln2_bias,
    w_gate,
    w_up,
    w_down,
    cotangent,
):
    full_float = jnp.float32
    bf16 = jnp.bfloat16
    group_rows = tokens.shape[0] * lax.axis_size("tp")
    local_heads = b_qkv.shape[1]
    local_width = local_heads * HEAD_DIM
    block_rows = min(512, group_rows)
    block_count = group_rows // block_rows
    scale = HEAD_DIM ** (-0.5)
    collected_rows = (
        lax.all_gather(ln1_gain, "fsdp", axis=0, tiled=True),
        lax.all_gather(ln1_bias, "fsdp", axis=0, tiled=True),
        lax.all_gather(w_qkv, "fsdp", axis=0, tiled=True),
        lax.all_gather(b_qkv, "fsdp", axis=2, tiled=True),
        lax.all_gather(w_out, "fsdp", axis=1, tiled=True),
        lax.all_gather(ln2_gain, "fsdp", axis=0, tiled=True),
        lax.all_gather(ln2_bias, "fsdp", axis=0, tiled=True),
        lax.all_gather(w_gate, "fsdp", axis=0, tiled=True),
        lax.all_gather(w_up, "fsdp", axis=0, tiled=True),
        lax.all_gather(w_down, "fsdp", axis=1, tiled=True),
    )
    inputs = tokens.astype(full_float)
    normed = layer_norm(
        inputs, collected_rows[0].astype(full_float), collected_rows[1].astype(full_float)
    ).astype(bf16)
    normed_every_row = lax.all_gather(normed, "tp", axis=0, tiled=True)
    projected_rows = jnp.einsum(
        "jf,fyk->jyk", normed_every_row, collected_rows[2], preferred_element_type=full_float
    )
    projected_rows = (
        projected_rows + collected_rows[3].astype(full_float).reshape(3, local_width)
    ).reshape(group_rows, 3, local_heads, HEAD_DIM)
    segment, position = slot_tables(seq_lens[0], group_rows)
    slot_ids = jnp.arange(group_rows, dtype=jnp.int32)
    queries = rotate(projected_rows[:, 0], position, ROT, 1.0).astype(bf16)
    key_rows = rotate(projected_rows[:, 1], position, ROT, 1.0).astype(bf16)
    value_rows = projected_rows[:, 2].astype(bf16)

    def block_scores(block):
        begin = block * block_rows
        stop = begin + block_rows
        scores = (
            jnp.einsum(
                "qhe,khe->hqk",
                queries[begin:stop],
                key_rows[:stop],
                preferred_element_type=full_float,
            )
            * scale
        )
        allowed = (segment[begin:stop][:, None] == segment[None, :stop]) & (
            slot_ids[None, :stop] <= slot_ids[begin:stop][:, None]
        )
        return jnp.where(allowed[None], scores, masked_value)

    outputs = []
    peaks = []
    totals = []
    for block in range(block_count):
        stop = (block + 1) * block_rows
        scores = block_scores(block)
        peak = jnp.max(scores, axis=-1, keepdims=True)
        weights = jnp.exp(scores - peak)
        total = jnp.sum(weights, axis=-1, keepdims=True)
        probability = (weights / total).astype(bf16)
        outputs.append(
            jnp.einsum(
                "hqk,khe->qhe", probability, value_rows[:stop], preferred_element_type=full_float
            ).astype(bf16)
        )
        peaks.append(peak)
        totals.append(total)
    attended = jnp.concatenate(outputs, axis=0).reshape(group_rows, local_width)
    partial_out = jnp.dot(attended, collected_rows[4], preferred_element_type=full_float)
    middle = inputs + lax.psum_scatter(
        partial_out.astype(jnp.bfloat16), "tp", scatter_dimension=0, tiled=True
    ).astype(jnp.float32)
    normed_two = layer_norm(
        middle, collected_rows[5].astype(full_float), collected_rows[6].astype(full_float)
    ).astype(bf16)
    normed_two_all = lax.all_gather(normed_two, "tp", axis=0, tiled=True)
    gate_value = jnp.dot(normed_two_all, collected_rows[7], preferred_element_type=full_float)
    up_value = jnp.dot(normed_two_all, collected_rows[8], preferred_element_type=full_float)
    sigmoid_gate = jax.nn.sigmoid(gate_value)
    hidden = (gate_value * sigmoid_gate * up_value).astype(bf16)
    down_part = jnp.dot(hidden, collected_rows[9], preferred_element_type=full_float)
    output = middle + lax.psum_scatter(
        down_part.astype(jnp.bfloat16), "tp", scatter_dimension=0, tiled=True
    ).astype(jnp.float32)
    second_gather = (
        lax.all_gather(ln1_gain, "fsdp", axis=0, tiled=True),
        lax.all_gather(ln1_bias, "fsdp", axis=0, tiled=True),
        lax.all_gather(w_qkv, "fsdp", axis=0, tiled=True),
        lax.all_gather(b_qkv, "fsdp", axis=2, tiled=True),
        lax.all_gather(w_out, "fsdp", axis=1, tiled=True),
        lax.all_gather(ln2_gain, "fsdp", axis=0, tiled=True),
        lax.all_gather(ln2_bias, "fsdp", axis=0, tiled=True),
        lax.all_gather(w_gate, "fsdp", axis=0, tiled=True),
        lax.all_gather(w_up, "fsdp", axis=0, tiled=True),
        lax.all_gather(w_down, "fsdp", axis=1, tiled=True),
    )
    grad_down = lax.all_gather(cotangent, "tp", axis=0, tiled=True)
    grad_hidden = jnp.einsum(
        "td,fd->tf", grad_down, second_gather[9], preferred_element_type=full_float
    )
    grad_w_down = jnp.einsum("tf,td->fd", hidden, grad_down, preferred_element_type=full_float)
    slope = sigmoid_gate + gate_value * sigmoid_gate * (1.0 - sigmoid_gate)
    grad_gate = (grad_hidden * up_value * slope).astype(bf16)
    grad_up = (grad_hidden * gate_value * sigmoid_gate).astype(bf16)
    grad_w_gate = jnp.einsum(
        "td,tf->df", normed_two_all, grad_gate, preferred_element_type=full_float
    )
    grad_w_up = jnp.einsum("td,tf->df", normed_two_all, grad_up, preferred_element_type=full_float)
    grad_norm_two = jnp.einsum(
        "tf,df->td", grad_gate, second_gather[7], preferred_element_type=full_float
    )
    grad_norm_two = grad_norm_two + jnp.einsum(
        "tf,df->td", grad_up, second_gather[8], preferred_element_type=full_float
    )
    grad_norm_two = lax.psum_scatter(
        grad_norm_two.astype(jnp.bfloat16), "tp", scatter_dimension=0, tiled=True
    ).astype(jnp.float32)
    unused_two, norm_back_two = jax.vjp(
        layer_norm, middle, second_gather[5].astype(full_float), second_gather[6].astype(full_float)
    )
    grad_middle_norm, grad_gain_two, grad_shift_two = norm_back_two(grad_norm_two)
    mlp_sums = (
        lax.psum_scatter(
            grad_gain_two.astype(jnp.bfloat16), "fsdp", scatter_dimension=0, tiled=True
        ).astype(jnp.float32),
        lax.psum_scatter(
            grad_shift_two.astype(jnp.bfloat16), "fsdp", scatter_dimension=0, tiled=True
        ).astype(jnp.float32),
        lax.psum_scatter(
            grad_w_gate.astype(jnp.bfloat16), "fsdp", scatter_dimension=0, tiled=True
        ).astype(jnp.float32),
        lax.psum_scatter(
            grad_w_up.astype(jnp.bfloat16), "fsdp", scatter_dimension=0, tiled=True
        ).astype(jnp.float32),
        lax.psum_scatter(
            grad_w_down.astype(jnp.bfloat16), "fsdp", scatter_dimension=1, tiled=True
        ).astype(jnp.float32),
    )
    grad_middle = cotangent.astype(full_float) + grad_middle_norm
    grad_branch = lax.all_gather(grad_middle.astype(bf16), "tp", axis=0, tiled=True)
    grad_attended = jnp.einsum(
        "td,ed->te", grad_branch, second_gather[4], preferred_element_type=full_float
    ).astype(bf16)
    grad_w_out = jnp.einsum("te,td->ed", attended, grad_branch, preferred_element_type=full_float)
    grad_attended = grad_attended.reshape(group_rows, local_heads, HEAD_DIM)
    grad_query_blocks = []
    grad_keys = jnp.zeros((group_rows, local_heads, HEAD_DIM), full_float)
    grad_values = jnp.zeros((group_rows, local_heads, HEAD_DIM), full_float)
    for block in range(block_count):
        begin = block * block_rows
        stop = begin + block_rows
        scores = block_scores(block)
        probability = jnp.exp(scores - peaks[block]) / totals[block]
        grad_rows = grad_attended[begin:stop]
        grad_prob = jnp.einsum(
            "qhe,khe->hqk", grad_rows, value_rows[:stop], preferred_element_type=full_float
        )
        inner = jnp.sum(probability * grad_prob, axis=-1, keepdims=True)
        grad_scores = (probability * (grad_prob - inner)).astype(bf16)
        grad_query_blocks.append(
            jnp.einsum(
                "hqk,khe->qhe", grad_scores, key_rows[:stop], preferred_element_type=full_float
            )
            * scale
        )
        grad_keys = grad_keys.at[:stop].add(
            jnp.einsum(
                "hqk,qhe->khe", grad_scores, queries[begin:stop], preferred_element_type=full_float
            )
            * scale
        )
        grad_values = grad_values.at[:stop].add(
            jnp.einsum(
                "hqk,qhe->khe",
                probability.astype(bf16),
                grad_rows,
                preferred_element_type=full_float,
            )
        )
    grad_queries = jnp.concatenate(grad_query_blocks, axis=0)
    projected_gradient = jnp.stack(
        [
            rotate(grad_queries, position, ROT, -1.0),
            rotate(grad_keys, position, ROT, -1.0),
            grad_values,
        ],
        axis=1,
    )
    projected_gradient = projected_gradient.astype(bf16).reshape(group_rows, 3, local_width)
    query_key_value_gradient = jnp.einsum(
        "xn,xfh->nfh", normed_every_row, projected_gradient, preferred_element_type=full_float
    )
    grad_b_qkv = jnp.sum(projected_gradient, axis=0, dtype=full_float).reshape(
        3, local_heads, HEAD_DIM
    )
    normed_gradient = jnp.einsum(
        "zyq,nyq->zn", projected_gradient, second_gather[2], preferred_element_type=full_float
    )
    normed_gradient = lax.psum_scatter(
        normed_gradient.astype(jnp.bfloat16), "tp", scatter_dimension=0, tiled=True
    ).astype(jnp.float32)
    unused_one, norm_back_one = jax.vjp(
        layer_norm, inputs, second_gather[0].astype(full_float), second_gather[1].astype(full_float)
    )
    grad_inputs_norm, grad_gain_one, grad_shift_one = norm_back_one(normed_gradient)
    attn_sums = (
        lax.psum_scatter(
            grad_gain_one.astype(jnp.bfloat16), "fsdp", scatter_dimension=0, tiled=True
        ).astype(jnp.float32),
        lax.psum_scatter(
            grad_shift_one.astype(jnp.bfloat16), "fsdp", scatter_dimension=0, tiled=True
        ).astype(jnp.float32),
        lax.psum_scatter(
            query_key_value_gradient.astype(jnp.bfloat16), "fsdp", scatter_dimension=0, tiled=True
        ).astype(jnp.float32),
        lax.psum_scatter(
            grad_b_qkv.astype(jnp.bfloat16), "fsdp", scatter_dimension=2, tiled=True
        ).astype(jnp.float32),
        lax.psum_scatter(
            grad_w_out.astype(jnp.bfloat16), "fsdp", scatter_dimension=1, tiled=True
        ).astype(jnp.float32),
    )
    norm_sums = lax.psum((attn_sums[0], attn_sums[1], mlp_sums[0], mlp_sums[1]), "tp")
    grad_inputs = grad_middle + grad_inputs_norm
    return (
        output.astype(bf16),
        grad_inputs,
        norm_sums[0],
        norm_sums[1],
        attn_sums[2],
        attn_sums[3],
        attn_sums[4],
        norm_sums[2],
        norm_sums[3],
        mlp_sums[2],
        mlp_sums[3],
        mlp_sums[4],
    )


def solution(mesh):
    placed = (
        P(("fsdp", "tp"), None),
        P("fsdp", None),
        P("fsdp"),
        P("fsdp"),
        P("fsdp", None, "tp"),
        P(None, "tp", "fsdp"),
        P("tp", "fsdp"),
        P("fsdp"),
        P("fsdp"),
        P("fsdp", "tp"),
        P("fsdp", "tp"),
        P("tp", "fsdp"),
        P(("fsdp", "tp"), None),
    )
    return jax.shard_map(
        local,
        mesh=mesh,
        in_specs=placed,
        out_specs=(
            P(("fsdp", "tp"), None),
            P(("fsdp", "tp"), None),
            P("fsdp"),
            P("fsdp"),
            P("fsdp", None, "tp"),
            P(None, "tp", "fsdp"),
            P("tp", "fsdp"),
            P("fsdp"),
            P("fsdp"),
            P("fsdp", "tp"),
            P("fsdp", "tp"),
            P("tp", "fsdp"),
        ),
        check_vma=False,
    )
```

profile of v0, /device:TPU:0, one launch (start us, length us, event | category | flops | bytes accessed | tf_op | source)
XLA Modules:
  0.0 1532.4 jit_solution(6159702881878681624)
XLA Ops:
  9.1 25.4 %all-gather = bf16[16,1,128]{2,1,0:T(2,128)(2,1)S(1)} all-gather(bf16[1,1,128]{2,1,0:T(2,128)(2,1)} %bitcast.139), channel_id=1, replica_groups=mesh['fsdp'=16,'tp'=8] {'fsdp'}, dimensions={0}, use_global_device_ids=true | all-gather | bytes 4352 | tf_op jit(solution)/shard_map/all_gather | solution.py:76
  34.5 19.3 %all-gather.1 = bf16[16,1,128]{2,1,0:T(2,128)(2,1)S(1)} all-gather(bf16[1,1,128]{2,1,0:T(2,128)(2,1)} %bitcast.140), channel_id=1, replica_groups=mesh['fsdp'=16,'tp'=8] {'fsdp'}, dimensions={0}, use_global_device_ids=true | all-gather | bytes 4352 | tf_op jit(solution)/shard_map/all_gather | solution.py:77
  60.0 22.4 %all_gather.53 = bf16[3,4,64]{1,0,2:T(4,128)(2,1)S(1)} all-gather(bf16[3,4,4]{1,0,2:T(4,128)(2,1)S(1)} %copy.71), channel_id=1, replica_groups=mesh['fsdp'=16,'tp'=8] {'fsdp'}, dimensions={2}, use_global_device_ids=true | all-gather | bytes 1632 | tf_op jit(solution)/shard_map/all_gather | solution.py:79
  84.3 74.0 %all-gather.14.cloned.1.call-done = bf16[1024,2048]{1,0:T(8,128)(2,1)} async-done(((bf16[128,2048]{1,0:T(8,128)(2,1)}), bf16[1024,2048]{1,0:T(8,128)(2,1)}) %all-gather.14.cloned.1.call-update) | async-done | bytes 4194320 | tf_op jit(solution)/shard_map/all_gather | solution.py:91
  180.7 27.9 %all-gather.18.cloned.1.call-done = bf16[256,2048]{1,0:T(8,128)(2,1)} async-done(((bf16[256,128]{1,0:T(8,128)(2,1)}), bf16[256,2048]{1,0:T(8,128)(2,1)}) %all-gather.18.cloned.1.call-update) | async-done | bytes 1048592 | tf_op jit(solution)/shard_map/all_gather | solution.py:80
  213.8 21.9 %all-gather.2 = bf16[16,1,128]{2,1,0:T(2,128)(2,1)S(1)} all-gather(bf16[1,1,128]{2,1,0:T(2,128)(2,1)S(1)} %bitcast.143), channel_id=1, replica_groups=mesh['fsdp'=16,'tp'=8] {'fsdp'}, dimensions={0}, use_global_device_ids=true | all-gather | bytes 4352 | tf_op jit(solution)/shard_map/all_gather | solution.py:81
  235.7 25.5 %all-gather.3 = bf16[16,1,128]{2,1,0:T(2,128)(2,1)S(1)} all-gather(bf16[1,1,128]{2,1,0:T(2,128)(2,1)S(1)} %bitcast.144), channel_id=1, replica_groups=mesh['fsdp'=16,'tp'=8] {'fsdp'}, dimensions={0}, use_global_device_ids=true | all-gather | bytes 4352 | tf_op jit(solution)/shard_map/all_gather | solution.py:82
  261.2 41.1 %reduce-scatter.19.cloned.1.call-done = bf16[128,2048]{1,0:T(8,128)(2,1)} async-done(((bf16[1024,2048]{1,0:T(8,128)(2,1)}), bf16[128,2048]{1,0:T(8,128)(2,1)}) %reduce-scatter.19.cloned.1.call-update) | async-done | bytes 524304 | tf_op jit(solution)/shard_map/reduce_scatter | solution.py:140
  309.4 49.1 %all-gather.24.cloned.1.call-done = bf16[2048,704]{0,1:T(8,128)(2,1)} async-done(((bf16[128,704]{0,1:T(8,128)(2,1)}), bf16[2048,704]{0,1:T(8,128)(2,1)}) %all-gather.24.cloned.1.call-update) | async-done | bytes 2883600 | tf_op jit(solution)/shard_map/all_gather | solution.py:84
  358.5 90.4 %all-gather.20.cloned.1.call-done = bf16[1024,2048]{1,0:T(8,128)(2,1)} async-done(((bf16[128,2048]{1,0:T(8,128)(2,1)}), bf16[1024,2048]{1,0:T(8,128)(2,1)}) %all-gather.20.cloned.1.call-update) | async-done | bytes 4194320 | tf_op jit(solution)/shard_map/all_gather | solution.py:146
  456.8 50.1 %all-gather.22.cloned.1.call-done = bf16[2048,704]{0,1:T(8,128)(2,1)} async-done(((bf16[128,704]{0,1:T(8,128)(2,1)}), bf16[2048,704]{0,1:T(8,128)(2,1)}) %all-gather.22.cloned.1.call-update) | async-done | bytes 2883600 | tf_op jit(solution)/shard_map/all_gather | solution.py:83
  514.7 46.1 %all-gather.26.cloned.1.call-done = bf16[704,2048]{1,0:T(8,128)(2,1)} async-done(((bf16[704,128]{1,0:T(8,128)(2,1)}), bf16[704,2048]{1,0:T(8,128)(2,1)}) %all-gather.26.cloned.1.call-update) | async-done | bytes 2883600 | tf_op jit(solution)/shard_map/all_gather | solution.py:85
  560.8 90.0 %all-gather.28.cloned.1.call-done = bf16[1024,2048]{1,0:T(8,128)(2,1)} async-done(((bf16[128,2048]{1,0:T(8,128)(2,1)}), bf16[1024,2048]{1,0:T(8,128)(2,1)}) %all-gather.28.cloned.1.call-update) | async-done | bytes 4194320 | tf_op jit(solution)/shard_map/all_gather | solution.py:167
  677.9 85.1 %reduce-scatter.23.cloned.1.call-done = bf16[128,2048]{1,0:T(8,128)(2,1)} async-done(((bf16[1024,2048]{1,0:T(8,128)(2,1)}), bf16[128,2048]{1,0:T(8,128)(2,1)}) %reduce-scatter.23.cloned.1.call-update) | async-done | bytes 524304 | tf_op jit(solution)/shard_map/reduce_scatter | solution.py:185
  765.8 91.0 %reduce-scatter.21.cloned.1.call-done = bf16[128,2048]{1,0:T(8,128)(2,1)} async-done(((bf16[1024,2048]{1,0:T(8,128)(2,1)}), bf16[128,2048]{1,0:T(8,128)(2,1)}) %reduce-scatter.21.cloned.1.call-update) | async-done | bytes 524304 | tf_op jit(solution)/shard_map/reduce_scatter | solution.py:152
  897.6 54.6 %all-gather.30.cloned.1.call-done = bf16[1024,2048]{1,0:T(8,128)(2,1)} async-done(((bf16[128,2048]{1,0:T(8,128)(2,1)}), bf16[1024,2048]{1,0:T(8,128)(2,1)}) %all-gather.30.cloned.1.call-update) | async-done | bytes 4194320 | tf_op jit(solution)/shard_map/all_gather | solution.py:210
  1013.7 20.4 %reduce-scatter.35.cloned.1.call-done = bf16[128,704]{1,0:T(8,128)(2,1)} async-done(((bf16[2048,704]{1,0:T(8,128)(2,1)}), bf16[128,704]{1,0:T(8,128)(2,1)}) %reduce-scatter.35.cloned.1.call-update) | async-done | bytes 180240
  1035.9 76.0 %reduce-scatter.31.cloned.1.call-done = bf16[128,704]{1,0:T(8,128)(2,1)} async-done(((bf16[2048,704]{1,0:T(8,128)(2,1)}), bf16[128,704]{1,0:T(8,128)(2,1)}) %reduce-scatter.31.cloned.1.call-update) | async-done | bytes 180240
  1113.8 76.0 %reduce-scatter.33.cloned.1.call-done = bf16[128,704]{1,0:T(8,128)(2,1)} async-done(((bf16[2048,704]{1,0:T(8,128)(2,1)}), bf16[128,704]{1,0:T(8,128)(2,1)}) %reduce-scatter.33.cloned.1.call-update) | async-done | bytes 180240
  1193.5 65.6 %reduce-scatter.29.cloned.1.call-done = bf16[128,256]{1,0:T(8,128)(2,1)} async-done(((bf16[2048,256]{1,0:T(8,128)(2,1)}), bf16[128,256]{1,0:T(8,128)(2,1)}) %reduce-scatter.29.cloned.1.call-update) | async-done | bytes 65552
  1260.7 77.0 %reduce-scatter.27.cloned.1.call-done = bf16[128,3,256]{2,0,1:T(8,128)(2,1)} async-done(((bf16[2048,3,256]{2,0,1:T(8,128)(2,1)}), bf16[128,3,256]{2,0,1:T(8,128)(2,1)}) %reduce-scatter.27.cloned.1.call-update) | async-done | bytes 196624 | tf_op jit(solution)/shard_map/reduce_scatter | solution.py:283
  1339.5 89.7 %reduce-scatter.25.cloned.1.call-done = bf16[128,2048]{1,0:T(8,128)(2,1)} async-done(((bf16[1024,2048]{1,0:T(8,128)(2,1)}), bf16[128,2048]{1,0:T(8,128)(2,1)}) %reduce-scatter.25.cloned.1.call-update) | async-done | bytes 524304 | tf_op jit(solution)/shard_map/reduce_scatter | solution.py:269
  1433.3 68.9 %all-reduce.8 = (bf16[2048]{0:T(1024)(128)(2,1)S(1)}, bf16[2048]{0:T(1024)(128)(2,1)S(1)}, bf16[2048]{0:T(1024)(128)(2,1)S(1)}, bf16[2048]{0:T(1024)(128)(2,1)S(1)}, bf16[3,4,64]{2,1,0:T(4,128)(2,1)S(1)}) all-reduce(bf16[2048]{0:T(1024)(128)(2,1)S(1)} %get-tuple-element.78, ...), channel_id=6, replica_groups=mesh['fsdp'=16,'tp'=8] {'fsdp'}, use_global_device_ids=true, to_apply=%region_22.23.clone | all-reduce | flops 8960 | bytes 35840
  1503.2 19.3 %all-reduce.7 = (f32[128]{0:T(128)}, f32[128]{0:T(128)}, f32[128]{0:T(128)}, f32[128]{0:T(128)}) all-reduce(f32[128]{0:T(128)S(1)} %dynamic-slice_convert_fusion.4, f32[128]{0:T(128)S(1)} %dynamic-slice_convert_fusion.3, f32[128]{0:T(128)S(1)} %dynamic-slice_convert_fusion.2, ...), channel_id=1, replica_groups=mesh['fsdp'=16,'tp'=8] {'tp'}, use_global_device_ids=true, to_apply=%region_23.24 | all-reduce | flops 512 | bytes 4096 | tf_op jit(solution)/shard_map/psum | solution.py:293
  (262 shorter events, 208.5 us)
Async XLA Ops:
  7.2 77.1 %all-gather.16.cloned.1.call-start = ((), (), s32[]{:S(2)}) async-start(), calls=%async_computation.10 | async-start | bytes 3342336 | tf_op jit(solution)/shard_map/all_gather | solution.py:78
  9.0 149.3 %all-gather.14.cloned.1.call-start = ((), (), s32[]{:S(2)}) async-start(), calls=%async_computation.9 | async-start | bytes 4718592 | tf_op jit(solution)/shard_map/all_gather | solution.py:91
  58.6 149.9 %all-gather.18.cloned.1.call-start = ((), (), s32[]{:S(2)}) async-start(), calls=%async_computation.11 | async-start | bytes 1114112 | tf_op jit(solution)/shard_map/all_gather | solution.py:80
  59.4 242.9 %reduce-scatter.19.cloned.1.call-start = ((), (), s32[]{:S(2)}) async-start(), calls=%async_computation.12 | async-start | bytes 4718592 | tf_op jit(solution)/shard_map/reduce_scatter | solution.py:140
  213.1 145.4 %all-gather.24.cloned.1.call-start = ((), (), s32[]{:S(2)}) async-start(), calls=%async_computation.15 | async-start | bytes 3063808 | tf_op jit(solution)/shard_map/all_gather | solution.py:84
  213.7 235.2 %all-gather.20.cloned.1.call-start = ((), (), s32[]{:S(2)}) async-start(), calls=%async_computation.13 | async-start | bytes 4718592 | tf_op jit(solution)/shard_map/all_gather | solution.py:146
  307.1 199.8 %all-gather.22.cloned.1.call-start = ((), (), s32[]{:S(2)}) async-start(), calls=%async_computation.14 | async-start | bytes 3063808 | tf_op jit(solution)/shard_map/all_gather | solution.py:83
  307.9 253.0 %all-gather.26.cloned.1.call-start = ((), (), s32[]{:S(2)}) async-start(), calls=%async_computation.16 | async-start | bytes 3063808 | tf_op jit(solution)/shard_map/all_gather | solution.py:85
  308.6 342.2 %all-gather.28.cloned.1.call-start = ((), (), s32[]{:S(2)}) async-start(), calls=%async_computation.18 | async-start | bytes 4718592 | tf_op jit(solution)/shard_map/all_gather | solution.py:167
  309.3 453.7 %reduce-scatter.23.cloned.1.call-start = ((), (), s32[]{:S(2)}) async-start(), calls=%async_computation.19 | async-start | bytes 4718592 | tf_op jit(solution)/shard_map/reduce_scatter | solution.py:185
  670.1 186.7 %reduce-scatter.21.cloned.1.call-start = ((), (), s32[]{:S(2)}) async-start(), calls=%async_computation.17 | async-start | bytes 4718592 | tf_op jit(solution)/shard_map/reduce_scatter | solution.py:152
  677.8 182.4 %copy-start.5 = (bf16[128,2048]{1,0:T(8,128)(2,1)S(1)}, bf16[128,2048]{1,0:T(8,128)(2,1)}, u32[]{:S(2)}) copy-start(bf16[128,2048]{1,0:T(8,128)(2,1)} %param.37) | copy-start | bytes 1572868
  677.9 274.3 %all-gather.30.cloned.1.call-start = ((), (), s32[]{:S(2)}) async-start(), calls=%async_computation.20 | async-start | bytes 4718592 | tf_op jit(solution)/shard_map/all_gather | solution.py:210
  861.3 172.8 %reduce-scatter.35.cloned.1.call-start = ((), (), s32[]{:S(2)}) async-start(), calls=%async_computation.26 | async-start | bytes 3342336
  873.3 238.7 %reduce-scatter.31.cloned.1.call-start = ((), (), s32[]{:S(2)}) async-start(), calls=%async_computation.24 | async-start | bytes 3342336
  885.3 304.5 %reduce-scatter.33.cloned.1.call-start = ((), (), s32[]{:S(2)}) async-start(), calls=%async_computation.25 | async-start | bytes 3342336
  897.5 361.6 %reduce-scatter.29.cloned.1.call-start = ((), (), s32[]{:S(2)}) async-start(), calls=%async_computation.23 | async-start | bytes 1114112
  988.8 348.9 %reduce-scatter.27.cloned.1.call-start = ((), (), s32[]{:S(2)}) async-start(), calls=%async_computation.22 | async-start | bytes 3342336 | tf_op jit(solution)/shard_map/reduce_scatter | solution.py:283
  1004.2 425.0 %reduce-scatter.25.cloned.1.call-start = ((), (), s32[]{:S(2)}) async-start(), calls=%async_computation.21 | async-start | bytes 4718592 | tf_op jit(solution)/shard_map/reduce_scatter | solution.py:269
  1011.2 418.0 %copy-start.28 = (f32[16,1,128]{2,1,0:T(1,128)S(1)}, f32[16,1,128]{2,1,0:T(1,128)}, u32[]{:S(2)}) copy-start(f32[16,1,128]{2,1,0:T(1,128)} %copy-done.27) | copy-start | bytes 24580
  1011.2 418.0 %copy-start.31 = (f32[128]{0:T(128)S(1)}, f32[128]{0:T(128)}, u32[]{:S(2)}) copy-start(f32[128]{0:T(128)} %copy-done.30) | copy-start | bytes 1540
  1035.2 395.4 %copy-start.47 = (f32[128]{0:T(128)S(1)}, f32[128]{0:T(128)}, u32[]{:S(2)}) copy-start(f32[128]{0:T(128)} %copy-done.46) | copy-start | bytes 1540
  1035.9 395.8 %copy-start.39 = (f32[128]{0:T(128)S(1)}, f32[128]{0:T(128)}, u32[]{:S(2)}) copy-start(f32[128]{0:T(128)} %copy-done.38) | copy-start | bytes 1540
  1191.0 331.6 %copy-start.3 = (f32[128,2048]{1,0:T(8,128)S(1)}, f32[128,2048]{1,0:T(8,128)}, u32[]{:S(2)}) copy-start(f32[128,2048]{1,0:T(8,128)} %copy-done.2) | copy-start | bytes 3145732
  (52 other events, 1134.1 us)
Sparse Core Ops, SparseCore 0:
  10.9 56.7 all-gather.15
  69.9 88.3 all-gather.13
  160.5 47.9 all-gather.17
  213.3 89.0 reduce-scatter.18
  304.4 54.0 all-gather.23
  360.6 88.3 all-gather.19
  451.2 55.6 all-gather.21
  509.1 51.6 all-gather.25
  562.5 88.3 all-gather.27
  670.2 92.8 reduce-scatter.22
  765.5 91.2 reduce-scatter.20
  861.4 90.7 all-gather.29
  956.2 77.8 reduce-scatter.34
  1038.0 73.9 reduce-scatter.30
  1115.8 73.9 reduce-scatter.32
  1193.6 65.5 reduce-scatter.28
  1263.5 74.1 reduce-scatter.26
  1340.1 88.9 reduce-scatter.24
where the time goes:
time: 1540 us; the launch traced here: 1530 us
  waiting for transfers between devices  1110 us (72%)
  blocking collectives  203 us (13%)
  matrix products  125 us (8%)
  other arithmetic  42.8 us (3%)
  local copies, waits for them, and re-layouts  35.7 us (2%)
  between operations  16.8 us (1%)
    unnamed x22, waiting for transfers between devices  241 us
    reduce_scatter x1, waiting for transfers between devices, local(): lax.psum_scatter(down_part.astype(jnp.bfloat16), 'tp', scatter_dimension=...  91 us
    all_gather x1, waiting for transfers between devices, local(): normed_two_all = lax.all_gather(normed_two, 'tp', axis=0, tiled=True)  90.4 us
    all_gather x1, waiting for transfers between devices, local(): grad_down = lax.all_gather(cotangent, 'tp', axis=0, tiled=True)  90 us
    reduce_scatter x1, waiting for transfers between devices, local(): lax.psum_scatter(normed_gradient.astype(jnp.bfloat16), 'tp', scatter_dime...  89.7 us
    reduce_scatter x1, waiting for transfers between devices, local(): lax.psum_scatter(grad_norm_two.astype(jnp.bfloat16), 'tp', scatter_dimens...  85.1 us
    reduce_scatter x1, waiting for transfers between devices, local(): lax.psum_scatter(query_key_value_gradient.astype(jnp.bfloat16), 'fsdp', s...  77 us
    all_gather x1, waiting for transfers between devices, local(): normed_every_row = lax.all_gather(normed, 'tp', axis=0, tiled=True)  74 us
  transfers between devices with their start and end apart: 18, of which 17 were waited for; matrix products, arithmetic and copies ran while one was open for 10% of the time, Pallas kernels for 0%

commit v1 on v0

v1 whole, which is shorter than its diff:
```python
import math

import jax
import jax.numpy as jnp
import numpy as np
from jax import lax
from jax.experimental import pallas as pl
from jax.experimental.pallas import tpu as pltpu
from jax.sharding import PartitionSpec as P

F32 = jnp.float32
BF16 = jnp.bfloat16
HEAD_DIM = 64
ROT = 16
EPS = 1e-05
ROPE_BASE = 10000.0
MASKED = -1e30
SCALE = HEAD_DIM**-0.5
ROWS_A = 1040
ROWS_Q = 784
ROWS_M = 704
MIB = 2**20


def nt(a, b):
    return lax.dot_general(a, b, (((1,), (1,)), ((), ())), preferred_element_type=F32)


def nn(a, b):
    return lax.dot_general(a, b, (((1,), (0,)), ((), ())), preferred_element_type=F32)


class Net:
    def __init__(self, send_sems, recv_sems, local_sems):
        f, t = lax.axis_index("fsdp"), lax.axis_index("tp")
        self.f, self.t = f, t
        self.x, self.zl = t // 2, lax.rem(t, 2)
        self.send_sems, self.recv_sems, self.local_sems = send_sems, recv_sems, local_sems
        self.started, self.pending, self.locals = 0, [], 0

    def tx(self, step, flip=0):
        zl = 1 - self.zl if flip else self.zl
        return lax.rem(self.x + step, 4) * 2 + zl

    def fy(self, f, step):
        return lax.rem(f + 4 * step, 16)

    def peer(self, name):
        if not isinstance(name, str):
            return name
        f, t = self.f, self.t
        core = f + 1 - 2 * lax.rem(f, 2)
        high = f + 2 - 4 * lax.rem(f // 2, 2)
        return {
            "xp": (f, self.tx(1)),
            "xm": (f, self.tx(3)),
            "zl": (f, self.tx(0, 1)),
            "zh": (high, t),
            "zo": (high, self.tx(0, 1)),
            "yp": (self.fy(f, 1), t),
            "ym": (self.fy(f, 3), t),
            "c": (core, t),
        }[name]

    def greet(self, names):
        barrier = pltpu.get_barrier_semaphore()
        for name in names:
            pl.semaphore_signal(
                barrier, inc=1, device_id=self.peer(name), device_id_type=pl.DeviceIdType.MESH
            )
        pl.semaphore_wait(barrier, len(names))

    def send(self, src, dst, name):
        k = self.started
        copy = pltpu.make_async_remote_copy(
            src_ref=src,
            dst_ref=dst,
            send_sem=self.send_sems.at[k],
            recv_sem=self.recv_sems.at[k],
            device_id=self.peer(name),
            device_id_type=pl.DeviceIdType.MESH,
        )
        copy.start()
        self.started += 1
        self.pending.append(copy)
        return copy

    def move(self, src, dst):
        copy = pltpu.make_async_copy(src, dst, self.local_sems.at[self.locals])
        copy.start()
        self.locals += 1
        return copy

    def settle(self, copies):
        for copy in copies:
            copy.wait_send()
        done = {id(copy) for copy in copies}
        self.pending = [copy for copy in self.pending if id(copy) not in done]

    def finish(self):
        for copy in self.pending:
            copy.wait_send()
        self.pending = []


class GatherTp:
    def __init__(self, net, src, buf):
        self.net, self.buf, self.src = net, buf, src
        half = src.shape[0] // 2
        self.lo, self.hi = pl.ds(0, half), pl.ds(half, half)

    def slot(self, step, flip=0):
        zl = 1 - self.net.zl if flip else self.net.zl
        return zl * 4 + lax.rem(self.net.x + step, 4)

    def pass_on(self, slot, rows, name):
        return self.net.send(self.buf.at[slot, rows], self.buf.at[slot, rows], name)

    def start(self):
        net, lo, hi = self.net, self.lo, self.hi
        own = self.slot(0)
        self.own = net.move(self.src, self.buf.at[own])
        self.xp_lo = net.send(self.src.at[lo], self.buf.at[own, lo], "xp")
        self.xm_hi = net.send(self.src.at[hi], self.buf.at[own, hi], "xm")
        self.xp_hi = net.send(self.src.at[hi], self.buf.at[own, hi], "xp")
        self.xm_lo = net.send(self.src.at[lo], self.buf.at[own, lo], "xm")

    def start_z(self):
        self.z = self.net.send(self.src, self.buf.at[self.slot(0)], "zl")

    def relay(self):
        lo, hi = self.lo, self.hi
        left, right = self.slot(3), self.slot(1)
        self.xp_lo.wait_recv()
        self.fwd_p = self.pass_on(left, lo, "xp")
        self.xm_hi.wait_recv()
        self.fwd_m = self.pass_on(right, hi, "xm")
        self.xp_hi.wait_recv()
        self.za_p = self.pass_on(left, hi, "zl")
        self.xm_lo.wait_recv()
        self.za_m = self.pass_on(right, lo, "zl")

    def relay_z(self):
        across = self.slot(0, 1)
        self.z.wait_recv()
        self.zb_p = self.pass_on(across, self.lo, "xp")
        self.zb_m = self.pass_on(across, self.hi, "xm")

    def relay_far(self):
        self.zb_p.wait_recv()
        self.fz_p = self.pass_on(self.slot(3, 1), self.lo, "xp")
        self.zb_m.wait_recv()
        self.fz_m = self.pass_on(self.slot(1, 1), self.hi, "xm")

    def plane(self):
        self.fwd_p.wait_recv()
        self.fwd_m.wait_recv()
        self.own.wait()

    def rest(self):
        for copy in (self.za_p, self.za_m, self.fz_p, self.fz_m):
            copy.wait_recv()


class GatherX:
    def __init__(self, net, src, buf):
        self.net, self.buf, self.src = net, buf, src
        self.half = src.shape[0] // 2

    def slot(self, step):
        return lax.rem(self.net.x + step, 4)

    def start(self):
        net, h = self.net, self.half
        lo, hi = pl.ds(0, h), pl.ds(h, h)
        own = self.slot(0)
        self.own = net.move(self.src, self.buf.at[own])
        self.xp_lo = net.send(self.src.at[lo], self.buf.at[own, lo], "xp")
        self.xm_hi = net.send(self.src.at[hi], self.buf.at[own, hi], "xm")
        self.xp_hi = net.send(self.src.at[hi], self.buf.at[own, hi], "xp")
        self.xm_lo = net.send(self.src.at[lo], self.buf.at[own, lo], "xm")

    def relay(self):
        net, h = self.net, self.half
        lo, hi = pl.ds(0, h), pl.ds(h, h)
        left, right = self.slot(3), self.slot(1)
        self.xp_lo.wait_recv()
        self.fwd_p = net.send(self.buf.at[left, lo], self.buf.at[left, lo], "xp")
        self.xm_hi.wait_recv()
        self.fwd_m = net.send(self.buf.at[right, hi], self.buf.at[right, hi], "xm")

    def near(self):
        self.xp_hi.wait_recv()
        self.xm_lo.wait_recv()

    def far(self):
        self.fwd_p.wait_recv()
        self.fwd_m.wait_recv()


class GatherW:
    def __init__(self, net, src, buf, wide, offset=0):
        self.net, self.src, self.buf, self.wide, self.offset = net, src, buf, wide, offset
        self.half = src.shape[0] // 32 * 16
        f = net.f
        high = f + 2 - 4 * lax.rem(f // 2, 2)
        self.sources = [((0, f), None), ((0, high), "zh")]
        if wide:
            self.sources += [((1, f), "zl"), ((1, high), "zo")]

    def at(self, key, step, rows=None):
        flip, f = key
        f = self.net.fy(f, step)
        start, size = (0, self.src.shape[0]) if rows is None else rows
        rows = pl.ds(self.offset + start, size)
        if self.wide:
            side = 1 - self.net.zl if flip else self.net.zl
            place = (f,) if len(self.buf.shape) == 4 else (f // 4, lax.rem(f // 2, 2), lax.rem(f, 2))
            return self.buf.at[(side, *place, rows)]
        return self.buf.at[f, rows]

    def pass_on(self, key, step, name, rows=None, src=None):
        here = self.at(key, step, rows)
        return self.net.send(here if src is None else src, here, name)

    def start(self):
        net, src = self.net, self.src
        own = (0, net.f)
        self.own = net.move(src, self.at(own, 0))
        self.by_z = [
            self.pass_on(own, 0, name, src=src) for _, name in self.sources if name is not None
        ]
        self.by_y = [(self.pass_on(own, 0, "yp", src=src), self.pass_on(own, 0, "ym", src=src))]
        self.by_c = [self.pass_on(own, 0, "c", src=src)]
        self.by_y2 = []

    def relay_z(self):
        for copy, (key, _) in zip(self.by_z, self.sources[1:]):
            copy.wait_recv()
            self.by_y.append((self.pass_on(key, 0, "yp"), self.pass_on(key, 0, "ym")))
            self.by_c.append(self.pass_on(key, 0, "c"))

    def relay_y(self, i):
        key, h = self.sources[i][0], self.half
        up, down = self.by_y[i]
        rows = self.src.shape[0]
        up.wait_recv()
        fwd_up = self.pass_on(key, 3, "yp", (0, h))
        down.wait_recv()
        fwd_down = self.pass_on(key, 1, "ym", (h, rows - h))
        self.by_c.append(self.pass_on(key, 3, "c"))
        self.by_c.append(self.pass_on(key, 1, "c"))
        self.by_y2.append((fwd_up, fwd_down))

    def relay_far(self, i):
        for copy in self.by_y2[i]:
            copy.wait_recv()
        self.by_c.append(self.pass_on(self.sources[i][0], 2, "c"))

    def finish(self):
        self.own.wait()
        for copy in self.by_c:
            copy.wait_recv()


def norm_rows(x, gain, bias):
    center = x - jnp.mean(x, axis=-1, keepdims=True)
    spread = jnp.mean(center * center, axis=-1, keepdims=True)
    return center * lax.rsqrt(spread + EPS) * gain + bias


def position_tables(lens_ref, begin_ref, cos_ref, sin_ref):
    rows = begin_ref.shape[0]
    slot = lax.broadcasted_iota(jnp.int32, (rows, 128), 0)
    begin = jnp.zeros((rows, 128), jnp.int32)
    end = jnp.int32(0)
    for i in range(lens_ref.shape[1]):
        length = lens_ref[0, i]
        end = end + length
        begin = begin + jnp.where(slot >= end, length, 0)
    begin_ref[...] = begin
    lane = lax.rem(lax.broadcasted_iota(jnp.int32, (1, 128), 1), HEAD_DIM)
    which = lax.rem(lane, ROT // 2)
    frequency = jnp.zeros((1, 128), F32)
    for j in range(ROT // 2):
        value = float(np.exp(np.float32(j) * np.float32(-2.0 * math.log(ROPE_BASE) / ROT)))
        frequency = jnp.where(which == j, value, frequency)
    angle = (slot - begin).astype(F32) * frequency
    turns = jnp.floor(angle * (2.0 / math.pi) + 0.5)
    r = angle - turns * 1.5703125 - turns * 4.837512969970703125e-4 - turns * 7.54978995489188216e-8
    z = r * r
    sine = ((-1.9515295891e-4 * z + 8.3321608736e-3) * z - 1.6666654611e-1) * z * r + r
    cosine = (
        ((2.443315711809948e-5 * z - 1.388731625493765e-3) * z + 4.166664568298827e-2) * z * z
        - 0.5 * z
        + 1.0
    )
    quadrant = turns - 4.0 * jnp.floor(turns * 0.25)
    odd = (quadrant == 1.0) | (quadrant == 3.0)
    cos_all = jnp.where(odd, sine, cosine)
    cos_all = jnp.where((quadrant == 1.0) | (quadrant == 2.0), -cos_all, cos_all)
    sin_all = jnp.where(odd, cosine, sine)
    sin_all = jnp.where(quadrant >= 2.0, -sin_all, sin_all)
    cos_ref[...] = jnp.where(lane < ROT, cos_all, 1.0)
    sin_ref[...] = jnp.where(lane < ROT, sin_all, 0.0)


def turn(values, cos, sin, direction):
    lane = lax.rem(lax.broadcasted_iota(jnp.int32, (1, 256), 1), HEAD_DIM)
    cos = jnp.concatenate([cos, cos], axis=1)
    sin = jnp.concatenate([sin, sin], axis=1) * direction
    after = pltpu.roll(values, 256 - ROT // 2, 1)
    before = pltpu.roll(values, ROT // 2, 1)
    other = jnp.where(lane < ROT // 2, -after, before)
    return values * cos + other * sin


def head_mask(h):
    return lax.broadcasted_iota(jnp.int32, (1, 256), 1) // HEAD_DIM == h


def scores_of(q_block, keys, begin, first, h):
    rows, stop = q_block.shape[0], keys.shape[0]
    q_head = jnp.where(head_mask(h), q_block, jnp.zeros_like(q_block))
    scores = nt(q_head, keys)
    key_slot = lax.broadcasted_iota(jnp.int32, (rows, stop), 1)
    query_slot = lax.broadcasted_iota(jnp.int32, (rows, stop), 0) + first
    return jnp.where((key_slot >= begin) & (key_slot <= query_slot), scores, MASKED)


def flip_into(ref, first, source):
    columns = source.shape[1]
    for begin in range(0, columns, 128):
        end = min(begin + 128, columns)
        ref[first + begin : first + end] = source[:, begin:end].T


def k1_kernel(
    x_ref, lens_ref, small_ref, w_qkv, w_out, pack_g, cot_ref,
    normed_hbm, wa_hbm, wg_hbm, cotg_hbm, q_hbm, k_hbm, v_hbm, att_hbm,
    normed_ref, wa_ref, wg_ref, cotg_ref, q_ref, k_ref, v_ref, att_ref,
    pack_a, raw, gains, biases, begin_ref, cos_ref, sin_ref, send_sems, recv_sems, local_sems,
):
    net = Net(send_sems, recv_sems, local_sems)
    pack_a[0:16] = small_ref[...]
    for j in range(3):
        flip_into(pack_a, 16 + 256 * j, w_qkv.at[j])
    net.greet(["xp", "xm", "zl", "zh", "zo", "yp", "ym", "c"])
    tokens = GatherTp(net, x_ref, raw)
    wa = GatherW(net, pack_a, wa_ref, False)
    wo = GatherW(net, w_out, wa_ref, False, ROWS_Q)
    wg = GatherW(net, pack_g, wg_ref, True)
    cot = GatherX(net, cot_ref, cotg_ref)
    wa.start()
    tokens.start()
    position_tables(lens_ref, begin_ref, cos_ref, sin_ref)
    wa.relay_z()
    tokens.start_z()
    wa.relay_y(0)
    tokens.relay()
    wa.relay_far(0)
    wa.relay_y(1)
    wg.start()
    wa.relay_far(1)
    tokens.relay_z()
    wa.finish()
    stores = []
    for f in range(16):
        small = wa_ref[f, 0:16].astype(F32)
        gains[0:2, f * 128 : (f + 1) * 128] = small[0:2]
        biases[0:16, :] = small if f == 0 else biases[0:16, :] + small

    def project(side):
        def norm_some(i, carry):
            values = raw[side * 4 + i].astype(F32)
            normed_ref[i * 2 + side] = norm_rows(values, gains[0:1, :], gains[1:2, :]).astype(BF16)
            return carry

        lax.fori_loop(0, 4, norm_some, 0)

        def some_rows(i, carry):
            chunks = [2 * (2 * i + n) + side for n in range(2)]
            given = jnp.concatenate([normed_ref[chunk] for chunk in chunks], axis=0)
            rows = [pl.ds(pl.multiple_of(chunk * 128, 128), 128) for chunk in chunks]
            cos = jnp.concatenate([cos_ref[r] for r in rows], axis=0)
            sin = jnp.concatenate([sin_ref[r] for r in rows], axis=0)
            for j, out in enumerate((q_ref, k_ref, v_ref)):
                lines = slice(16 + 256 * j, 16 + 256 * (j + 1))
                total = nt(given, jnp.concatenate([wa_ref[f, lines] for f in range(16)], axis=1))
                total = total + jnp.concatenate([biases[4 + 2 * j : 5 + 2 * j], biases[5 + 2 * j : 6 + 2 * j]], axis=1)
                if j < 2:
                    total = turn(total, cos, sin, 1.0)
                for n in range(2):
                    out[rows[n]] = total[n * 128 : (n + 1) * 128].astype(BF16)
            return carry

        lax.fori_loop(0, 2, some_rows, 0)

    tokens.plane()
    wg.relay_y(0)
    project(net.zl)
    tokens.relay_far()
    wo.start()
    wg.relay_z()
    cot.start()
    wg.relay_far(0)
    tokens.rest()
    project(1 - net.zl)
    stores += [net.move(normed_ref, normed_hbm), net.move(q_ref, q_hbm)]
    stores += [net.move(k_ref, k_hbm), net.move(v_ref, v_hbm)]
    wg.relay_y(1)
    for block in range(4):
        first, stop = block * 256, (block + 1) * 256
        q_block = q_ref[first:stop] * jnp.asarray(SCALE, BF16)
        begin = begin_ref[first:stop, 0:1]
        mixed = jnp.zeros((256, 256), F32)
        for h in range(4):
            scores = scores_of(q_block, k_ref[0:stop], begin, first, h)
            weights = jnp.exp(scores - jnp.max(scores, axis=-1, keepdims=True))
            probs = (weights * (1.0 / jnp.sum(weights, axis=-1, keepdims=True))).astype(BF16)
            mixed = jnp.where(head_mask(h), nn(probs, v_ref[0:stop]), mixed)
        att_ref[first:stop] = mixed.astype(BF16)
        if block == 1:
            wg.relay_y(2)
            wo.relay_z()
        if block == 2:
            wg.relay_y(3)
            wg.relay_far(1)
            wo.relay_y(0)
    stores.append(net.move(att_ref, att_hbm))
    cot.relay()
    wo.relay_y(1)
    wg.relay_far(2)
    wg.relay_far(3)
    wo.relay_far(0)
    wo.relay_far(1)
    wg.finish()
    stores.append(net.move(wg_ref, wg_hbm))
    wo.finish()
    stores.append(net.move(wa_ref, wa_hbm))
    cot.own.wait()
    cot.near()
    cot.far()
    stores.append(net.move(cotg_ref, cotg_hbm))
    for copy in stores:
        copy.wait()
    net.finish()


def hbm(shape, dtype=BF16):
    return jax.ShapeDtypeStruct(shape, dtype)


VM = pl.BlockSpec(memory_space=pltpu.VMEM)
SM = pl.BlockSpec(memory_space=pltpu.SMEM)
AN = pl.BlockSpec(memory_space=pl.ANY)


def k1(x, lens, small, w_qkv, w_out, pack_g, cot):
    shapes = [
        (8, 128, 2048), (16, ROWS_A, 128), (2, 16, ROWS_M, 128), (4, 128, 2048),
        (1024, 256), (1024, 256), (1024, 256), (1024, 256),
    ]
    return pl.pallas_call(
        k1_kernel,
        out_shape=[hbm(s) for s in shapes],
        in_specs=[VM, SM, VM, VM, VM, VM, VM],
        out_specs=[AN] * 8,
        scratch_shapes=[pltpu.VMEM(s, BF16) for s in shapes + [(ROWS_Q, 128)]]
        + [
            pltpu.VMEM((8, 128, 2048), BF16),
            pltpu.VMEM((8, 2048), F32),
            pltpu.VMEM((16, 128), F32),
            pltpu.VMEM((1024, 128), jnp.int32),
            pltpu.VMEM((1024, 128), F32),
            pltpu.VMEM((1024, 128), F32),
            pltpu.SemaphoreType.DMA((160,)),
            pltpu.SemaphoreType.DMA((160,)),
            pltpu.SemaphoreType.DMA((16,)),
        ],
        compiler_params=pltpu.CompilerParams(
            collective_id=1, has_side_effects=True, vmem_limit_bytes=56 * MIB
        ),
        name="gather_project_attend",
    )(x, lens, small, w_qkv, w_out, pack_g, cot)


def small_rows(ln1_gain, ln1_bias, b_qkv, ln2_gain, ln2_bias):
    spread = jnp.zeros((3, 4, 16, 4), BF16)
    spread = lax.dynamic_update_slice(
        spread, b_qkv.reshape(3, 4, 1, 4), (0, 0, lax.axis_index("fsdp"), 0)
    ).reshape(6, 128)
    rows = lax.broadcasted_iota(jnp.int32, (16, 128), 0)
    small = jnp.pad(spread, ((4, 6), (0, 0)))
    for i, row in enumerate((ln1_gain, ln1_bias, ln2_gain, ln2_bias)):
        small = jnp.where(rows == i, row[None, :], small)
    return small


class ScatterTp:
    def __init__(self, net, parts, got, got_half):
        self.net, self.parts, self.got, self.got_half = net, parts, got, got_half
        half = parts.shape[1] // 2
        self.lo, self.hi = pl.ds(0, half), pl.ds(half, half)

    slot = GatherTp.slot

    def half_to(self, slot, rows, name, place):
        return self.net.send(self.parts.at[slot, rows], self.got_half.at[place], name)

    def add(self, slot, rows, *places):
        total = self.parts[slot, rows].astype(F32)
        for place in places:
            total = total + self.got_half[place].astype(F32)
        self.parts[slot, rows] = total.astype(BF16)

    def start_side(self):
        lo, hi = self.lo, self.hi
        self.zx2 = [self.half_to(self.slot(2, 1), lo, "xm", 0), self.half_to(self.slot(2, 1), hi, "xp", 1)]
        self.by_z = [self.half_to(self.slot(3, 1), hi, "zl", 2), self.half_to(self.slot(1, 1), lo, "zl", 4)]

    def start_plane(self):
        net, parts, lo, hi = self.net, self.parts, self.lo, self.hi
        far, left, right = self.slot(2), self.slot(3), self.slot(1)
        self.x2 = [self.half_to(far, hi, "xm", 6), self.half_to(far, lo, "xp", 7)]
        self.near_m = [net.send(parts.at[left, lo], self.got.at[1, lo], "xm")]
        self.near_p = [net.send(parts.at[right, hi], self.got.at[2, hi], "xp")]

    def relay_side(self):
        lo, hi = self.lo, self.hi
        self.zx2[0].wait_recv()
        self.add(self.slot(3, 1), lo, 0)
        self.across = [self.half_to(self.slot(3, 1), lo, "xm", 3)]
        self.zx2[1].wait_recv()
        self.add(self.slot(1, 1), hi, 1)
        self.across.append(self.half_to(self.slot(1, 1), hi, "xp", 5))

    def relay_across(self):
        across = self.slot(0, 1)
        self.across[0].wait_recv()
        self.add(across, self.lo, 3)
        self.across[1].wait_recv()
        self.add(across, self.hi, 5)
        self.z_own = self.net.send(self.parts.at[across], self.got.at[0], "zl")

    def relay_near(self):
        net, parts, lo, hi = self.net, self.parts, self.lo, self.hi
        left, right = self.slot(3), self.slot(1)
        self.by_z[0].wait_recv()
        self.x2[0].wait_recv()
        self.add(left, hi, 2, 6)
        self.near_m.append(net.send(parts.at[left, hi], self.got.at[1, hi], "xm"))
        self.by_z[1].wait_recv()
        self.x2[1].wait_recv()
        self.add(right, lo, 4, 7)
        self.near_p.append(net.send(parts.at[right, lo], self.got.at[2, lo], "xp"))

    def wait(self):
        self.z_own.wait_recv()
        for copy in self.near_p + self.near_m:
            copy.wait_recv()

    def total(self):
        total = self.parts[self.slot(0)].astype(F32)
        for i in range(3):
            total = total + self.got[i].astype(F32)
        return total


class ScatterX:
    def __init__(self, net, parts, got, got_half):
        self.net, self.parts, self.got, self.got_half = net, parts, got, got_half
        self.half = parts.shape[1] // 2

    slot = GatherX.slot

    def add(self, slot, rows, arrived):
        total = self.parts[slot, rows].astype(F32) + arrived[...].astype(F32)
        self.parts[slot, rows] = total.astype(BF16)

    def start_far(self):
        net, h, parts = self.net, self.half, self.parts
        far = self.slot(2)
        self.half_p = net.send(parts.at[far, pl.ds(0, h)], self.got_half.at[0], "xp")
        self.half_m = net.send(parts.at[far, pl.ds(h, h)], self.got_half.at[1], "xm")

    def start_near(self):
        net, h, parts = self.net, self.half, self.parts
        right, left = self.slot(1), self.slot(3)
        self.near_p = [net.send(parts.at[right, pl.ds(h, h)], self.got.at[0, pl.ds(h, h)], "xp")]
        self.near_m = [net.send(parts.at[left, pl.ds(0, h)], self.got.at[1, pl.ds(0, h)], "xm")]

    def relay_near(self):
        net, h, parts = self.net, self.half, self.parts
        right, left = self.slot(1), self.slot(3)
        self.half_p.wait_recv()
        self.add(right, pl.ds(0, h), self.got_half.at[0])
        self.near_p.append(net.send(parts.at[right, pl.ds(0, h)], self.got.at[0, pl.ds(0, h)], "xp"))
        self.half_m.wait_recv()
        self.add(left, pl.ds(h, h), self.got_half.at[1])
        self.near_m.append(net.send(parts.at[left, pl.ds(h, h)], self.got.at[1, pl.ds(h, h)], "xm"))

    def wait(self):
        for copy in self.near_p + self.near_m:
            copy.wait_recv()

    def total(self):
        total = self.parts[self.slot(0)].astype(F32)
        return total + self.got[0].astype(F32) + self.got[1].astype(F32)


def side_by_side(ref, lead, lines, slabs):
    return jnp.concatenate([ref[(*lead, f, lines)] for f in slabs], axis=1)


TILES = ((0, 256), (256, 512), (512, 704))


def k2_kernel(
    x_ref, att_ref, wa_hbm, wg_hbm, pack_u, pack_d, cot_ref, cotg_hbm,
    middle_hbm, gmid_ref, down_hbm, grads_hbm, ln2_ref,
    wo, small_ref, middle_ref, down_ref, parts, got8, got8_half, gains, n2_own, n2, wg, wu, wd, cotg, gate, up, ghid, hid, gg, gu, got4, got4_half, flipped,
    send_sems, recv_sems, local_sems,
):
    net = Net(send_sems, recv_sems, local_sems)
    net.greet(["xp", "xm", "zl", "zh", "zo", "yp", "ym", "c"])
    wug = GatherW(net, pack_u, wu, True)
    wdg = GatherW(net, pack_d, wd, True)
    wdg.start()
    first = [net.move(wa_hbm.at[:, pl.ds(784, 256)], wo), net.move(wa_hbm.at[:, pl.ds(0, 16)], small_ref)]
    moves = [net.move(wg_hbm, wg), net.move(cotg_hbm, cotg)]
    for copy in first:
        copy.wait()
    sum8 = ScatterTp(net, parts, got8, got8_half)

    def attention_out(side):
        rows = [att_ref[pl.ds(pl.multiple_of((2 * i + side) * 128, 128), 128)] for i in range(4)]
        rows = jnp.concatenate(rows, axis=0)
        for pair in range(8):
            weight = side_by_side(wo, (), slice(0, 256), (2 * pair, 2 * pair + 1))
            part = nn(rows, weight).astype(BF16).reshape(4, 128, 256)
            parts[pl.ds(side * 4, 4), :, pair * 256 : (pair + 1) * 256] = part

    attention_out(1 - net.zl)
    sum8.start_side()
    attention_out(net.zl)
    for f in range(16):
        small = small_ref[f].astype(F32)
        gains[0:2, f * 128 : (f + 1) * 128] = small[2:4]
    sum8.start_plane()
    sum8.relay_side()
    wdg.relay_z()
    wug.start()
    wdg.relay_y(0)
    sum8.relay_across()
    for i in range(1, 4):
        wdg.relay_y(i)
    wug.relay_z()
    sum8.relay_near()
    for i in range(4):
        wdg.relay_far(i)
    wug.relay_y(0)
    sum8.wait()
    middle = x_ref[...].astype(F32) + sum8.total()
    middle_ref[...] = middle
    n2_own[...] = norm_rows(middle, gains[0:1], gains[1:2]).astype(BF16)
    gather = GatherX(net, n2_own, n2)
    gather.start()
    stores = [net.move(middle_ref, middle_hbm)]
    for copy in moves:
        copy.wait()
    for i in range(1, 4):
        wug.relay_y(i)
    wdg.finish()

    def rows_of(slot):
        return pl.ds(slot * 128 if isinstance(slot, int) else pl.multiple_of(slot * 128, 128), 128)

    def grad_hidden(slots):
        given = jnp.concatenate([cotg[slot] for slot in slots], axis=0)
        for side in range(2):
            for a, b in TILES:
                value = nt(given, side_by_side(wd, (side,), slice(a, b), range(16))).astype(BF16)
                for i, slot in enumerate(slots):
                    ghid[side, rows_of(slot), a:b] = value[i * 128 : (i + 1) * 128]

    def project(slots, weight, out):
        given = jnp.concatenate([n2[slot] for slot in slots], axis=0)
        for side in range(2):
            for a, b in TILES:
                value = nt(given, side_by_side(weight, (side,), slice(a, b), range(16)))
                for i, slot in enumerate(slots):
                    out[side, rows_of(slot), a:b] = value[i * 128 : (i + 1) * 128]

    def units(slots):
        for slot in slots:
            rows = rows_of(slot)
            for side in range(2):
                g, u = gate[side, rows], up[side, rows]
                gh = ghid[side, rows].astype(F32)
                sig = 1.0 / (1.0 + jnp.exp(-g))
                act = g * sig
                hid[side, rows] = (act * u).astype(BF16)
                gu[side, rows] = (gh * act).astype(BF16)
                gg[side, rows] = (gh * u * (sig + act * (1.0 - sig))).astype(BF16)

    grad_parts = parts.at[pl.ds(0, 4)]

    def back(slots):
        rows = [rows_of(slot) for slot in slots]
        given = [
            (jnp.concatenate([ref[side, r] for r in rows], axis=0), weight, side)
            for ref, weight in ((gg, wg), (gu, wu))
            for side in range(2)
        ]
        for pair in range(8):
            total = None
            for value, weight, side in given:
                term = nn(value, side_by_side(weight, (side,), slice(0, 704), (2 * pair, 2 * pair + 1)))
                total = term if total is None else total + term
            for i, slot in enumerate(slots):
                grad_parts[slot, :, pair * 256 : (pair + 1) * 256] = total[i * 128 : (i + 1) * 128].astype(BF16)

    own, right, far, left = (gather.slot(i) for i in range(4))
    grad_hidden([0, 1, 2, 3])
    gather.relay()
    gather.own.wait()
    project([own], wg, gate)
    for i in range(4):
        wug.relay_far(i)
    gather.near()
    project([right, left], wg, gate)
    gather.far()
    project([far], wg, gate)
    wug.finish()
    project([0, 1, 2, 3], wu, up)
    sum4 = ScatterX(net, grad_parts, got4, got4_half)
    net.finish()
    units([far])
    back([far])
    sum4.start_far()
    units([right, left])
    back([right, left])
    sum4.start_near()
    units([own])
    back([own])
    sum4.relay_near()

    def down(m, carry):
        rows = pl.ds(pl.multiple_of(m * 256, 256), 256)
        for pair in range(8):
            total = None
            for side in range(2):
                term = nn(hid[side, rows], side_by_side(wd, (side,), slice(0, 704), (2 * pair, 2 * pair + 1)))
                total = term if total is None else total + term
            down_ref[pl.ds(2 * m, 2), :, pair * 256 : (pair + 1) * 256] = total.astype(BF16).reshape(2, 128, 256)
        return carry

    lax.fori_loop(0, 2, down, 0)
    stores.append(net.move(down_ref, down_hbm))
    for k, (ref, given, weight) in enumerate(((gg, n2, wg), (gu, n2, wu), (hid, cotg, wd))):
        for side in range(2):
            flipped[...] = ref[side].T
            for pair in range(8):
                some = given[:, :, pair * 256 : (pair + 1) * 256].reshape(512, 256)
                product = nn(flipped[...], some).astype(BF16)
                weight[side, 2 * pair] = product[:, 0:128]
                weight[side, 2 * pair + 1] = product[:, 128:256]
            stores.append(net.move(weight.at[side], grads_hbm.at[k, side]))
    sum4.wait()

    given = sum4.total()
    grad, normed = norm_back(middle_ref[...], given, gains[0:1])
    gmid_ref[...] = cot_ref[...].astype(F32) + grad
    ln2_ref[0:1] = jnp.sum(given * normed, axis=0, keepdims=True)
    ln2_ref[1:2] = jnp.sum(given, axis=0, keepdims=True)
    ln2_ref[2:8] = jnp.zeros((6, 2048), F32)
    for copy in stores:
        copy.wait()
    net.finish()


def norm_back(x, given, gain):
    center = x - jnp.mean(x, axis=-1, keepdims=True)
    scale = lax.rsqrt(jnp.mean(center * center, axis=-1, keepdims=True) + EPS)
    normed = center * scale
    q = given * gain
    grad = scale * (
        q - jnp.mean(q, axis=-1, keepdims=True) - normed * jnp.mean(q * normed, axis=-1, keepdims=True)
    )
    return grad, normed


def k2(x, att, wa, wg, pack_u, pack_d, cot, cotg):
    shapes = [
        ((128, 2048), F32, AN), ((128, 2048), F32, VM), ((4, 128, 2048), BF16, AN),
        ((3, 2, 16, ROWS_M, 128), BF16, AN), ((8, 2048), F32, VM),
    ]
    wide, tall = (2, 16, ROWS_M, 128), (2, 512, ROWS_M)
    return pl.pallas_call(
        k2_kernel,
        out_shape=[jax.ShapeDtypeStruct(s, d) for s, d, _ in shapes],
        in_specs=[VM, VM, AN, AN, VM, VM, VM, AN],
        out_specs=[m for _, _, m in shapes],
        scratch_shapes=[
            pltpu.VMEM((16, 256, 128), BF16),
            pltpu.VMEM((16, 16, 128), BF16),
            pltpu.VMEM((128, 2048), F32),
            pltpu.VMEM((4, 128, 2048), BF16),
            pltpu.VMEM((8, 128, 2048), BF16),
            pltpu.VMEM((3, 128, 2048), BF16),
            pltpu.VMEM((8, 64, 2048), BF16),
            pltpu.VMEM((8, 2048), F32),
            pltpu.VMEM((128, 2048), BF16),
            pltpu.VMEM((4, 128, 2048), BF16),
            pltpu.VMEM(wide, BF16),
            pltpu.VMEM(wide, BF16),
            pltpu.VMEM(wide, BF16),
            pltpu.VMEM((4, 128, 2048), BF16),
            pltpu.VMEM(tall, F32),
            pltpu.VMEM(tall, F32),
            pltpu.VMEM(tall, BF16),
            pltpu.VMEM(tall, BF16),
            pltpu.VMEM(tall, BF16),
            pltpu.VMEM(tall, BF16),
            pltpu.VMEM((2, 128, 2048), BF16),
            pltpu.VMEM((2, 64, 2048), BF16),
            pltpu.VMEM((ROWS_M, 512), BF16),
            pltpu.SemaphoreType.DMA((160,)),
            pltpu.SemaphoreType.DMA((160,)),
            pltpu.SemaphoreType.DMA((16,)),
        ],
        compiler_params=pltpu.CompilerParams(
            collective_id=2, has_side_effects=True, vmem_limit_bytes=62 * MIB
        ),
        name="project_norm_feed_forward",
    )(x, att, wa, wg, pack_u, pack_d, cot, cotg)


def tn(a, b):
    return lax.dot_general(a, b, (((0,), (0,)), ((), ())), preferred_element_type=F32)


class ScatterW:
    def __init__(self, net, rows, own, theirs, far, near):
        self.net, self.rows, self.half = net, rows, rows // 2
        self.own, self.theirs, self.far, self.near = own, theirs, far, near
        self.y = net.f // 4

    def at(self, step):
        return lax.rem(self.y + step, 4)

    def add(self, target, rows, *arrived):
        if len(arrived) == 1:
            target[:, rows] = target[:, rows] + arrived[0]
            return
        total = target[:, rows].astype(F32)
        for value in arrived:
            total = total + value.astype(F32)
        target[:, rows] = total.astype(BF16)

    def step_a(self):
        net, h, rows = self.net, self.half, self.rows
        lo, hi = pl.ds(0, h), pl.ds(h, rows - h)
        own, y = self.own, self.at

        def add(step):
            ref = self.theirs(y(step))
            self.add(own(y(step)), pl.ds(0, rows), ref[...])

        add(2)
        self.far_p = net.send(own(y(2)).at[:, lo], self.far.at[0], "yp")
        self.far_m = net.send(own(y(2)).at[:, hi], self.far.at[1], "ym")
        add(1)
        self.near_p = [net.send(own(y(1)).at[:, hi], self.near.at[0, :, hi], "yp")]
        add(3)
        self.near_m = [net.send(own(y(3)).at[:, lo], self.near.at[1, :, lo], "ym")]
        add(0)

    def step_b(self):
        net, h, rows = self.net, self.half, self.rows
        lo, hi = pl.ds(0, h), pl.ds(h, rows - h)
        own, y, far = self.own, self.at, self.far
        self.far_p.wait_recv()
        self.add(own(y(1)), lo, far[0])
        self.near_p.append(net.send(own(y(1)).at[:, lo], self.near.at[0, :, lo], "yp"))
        self.far_m.wait_recv()
        self.add(own(y(3)), hi, far[1])
        self.near_m.append(net.send(own(y(3)).at[:, hi], self.near.at[1, :, hi], "ym"))

    def step_c(self):
        for copy in self.near_p + self.near_m:
            copy.wait_recv()
        near = self.near
        self.add(self.own(self.y), pl.ds(0, self.rows), near[0], near[1])


def k3_kernel(
    x_ref, lens_ref, wa_hbm, gmid_ref, middle_hbm, down_hbm, ln2_ref, grads_hbm, normed_hbm, q_hbm, k_hbm, v_hbm, att_hbm,
    out_ref, dtok_ref, dm_ref, da_ref, small_ref, theirs_hbm,
    q_ref, k_ref, v_ref, att_ref, wa, gb, parts, got8, got8_half, got4, got4_half, g_own, gains, ga, dk, dv, gproj, flipped, begin_ref, cos_ref, sin_ref,
    sums, stage, far_m, near_m, by_z, theirs_a, far_a, near_a, by_z_a, small_out, small_in, small_tp, small_got,
    send_sems, recv_sems, local_sems,
):
    net = Net(send_sems, recv_sems, local_sems)
    f, t = net.f, net.t
    core, zh, y = lax.rem(f, 2), lax.rem(f // 2, 2), f // 4
    across_f = [(lax.rem(f + i, 16), t) for i in range(1, 16)]
    across_t = [(f, lax.rem(t + j, 8)) for j in range(1, 8)]
    net.greet(across_f + across_t + ["zo"])
    load_wa = net.move(wa_hbm, wa)
    units = [(k, flip) for k in range(3) for flip in (1, 0)]
    sides = (net.zl, 1 - net.zl)
    to_core, load_sums = [], []
    for u, (k, flip) in enumerate(units):
        there = stage.at[u] if u < 2 else theirs_hbm.at[u]
        to_core.append(net.send(grads_hbm.at[k, sides[flip], :, :, 1 - core], there, "c"))
        load_sums.append(net.move(grads_hbm.at[k, sides[flip], :, :, core], sums.at[u]))
    down = parts.at[pl.ds(net.zl * 4, 4)]
    load_down = net.move(down_hbm, down)
    load_rest = [net.move(q_hbm, q_ref), net.move(k_hbm, k_ref), net.move(v_hbm, v_ref), net.move(att_hbm, att_ref)]
    load_middle = net.move(middle_hbm, dtok_ref)

    def cast(i, carry):
        rows = pl.ds(pl.multiple_of(i * 32, 32), 32)
        g_own[rows] = gmid_ref[rows].astype(BF16)
        return carry

    lax.fori_loop(0, 4, cast, 0)
    gather = GatherTp(net, g_own, gb)
    gather.start()
    gather.start_z()
    position_tables(lens_ref, begin_ref, cos_ref, sin_ref)
    load_wa.wait()
    for i in range(16):
        small = wa[i // 4, i // 2 % 2, i % 2, 0:16].astype(F32)
        gains[0:2, i * 128 : (i + 1) * 128] = small[0:2]

    def unit(u):
        return ScatterW(
            net, ROWS_M, lambda yy: sums.at[u, yy], lambda yy: stage.at[u % 2, yy], far_m.at[u], near_m.at[u]
        )

    scatter = [unit(u) for u in range(6)]
    z_copies = [[] for _ in range(3)]

    staged = []

    def bring(u):
        to_core[u].wait_recv()
        staged.append(net.move(theirs_hbm.at[u], stage.at[u % 2]))

    def step_a(u):
        if u < 2:
            to_core[u].wait_recv()
        else:
            staged[u - 2].wait()
        load_sums[u].wait()
        scatter[u].step_a()
        if u < 4:
            bring(u + 2)

    def step_b(u):
        scatter[u].step_b()

    def step_c(u):
        k, flip = units[u]
        scatter[u].step_c()
        if flip:
            z_copies[k].append(net.send(sums.at[u, y, zh], by_z.at[k, 1], "zl"))
            z_copies[k].append(net.send(sums.at[u, y, 1 - zh], by_z.at[k, 2], "zo"))
        else:
            z_copies[k].append(net.send(sums.at[u, y, 1 - zh], by_z.at[k, 0], "zh"))

    def step_d(k):
        for copy in z_copies[k]:
            copy.wait_recv()

        total = sums[2 * k + 1, y, zh].astype(F32)
        for j in range(3):
            total = total + by_z[k, j].astype(F32)
        dm_ref[k] = total

    def attended_back(side):
        given = gb[pl.ds(side * 4, 4)].reshape(512, 2048)
        weight = jnp.concatenate([wa[i // 4, i // 2 % 2, i % 2, 784:1040] for i in range(16)], axis=1)
        value = nt(given, weight).astype(BF16)
        for i in range(4):
            ga[pl.ds(pl.multiple_of((2 * i + side) * 128, 128), 128)] = value[i * 128 : (i + 1) * 128]

    step_a(0)
    step_a(1)
    gather.relay()
    gather.relay_z()
    step_a(2)
    step_b(0)
    gather.relay_far()
    gather.plane()
    attended_back(net.zl)
    step_a(3)
    step_b(1)
    gather.rest()
    attended_back(1 - net.zl)
    load_down.wait()
    sum4 = ScatterX(net, down, got4, got4_half)
    sum4.start_far()
    sum4.start_near()
    for copy in load_rest:
        copy.wait()
    dk[...] = jnp.zeros_like(dk)
    dv[...] = jnp.zeros_like(dv)

    def attention_back(block):
        first, stop = block * 256, (block + 1) * 256
        q_block = q_ref[first:stop] * jnp.asarray(SCALE, BF16)
        ga_block = ga[first:stop]
        begin = begin_ref[first:stop, 0:1]
        dq = jnp.zeros((256, 256), F32)
        many_q, many_g, many_p, many_s = [], [], [], []
        for h in range(4):
            mask = head_mask(h)
            g_head = jnp.where(mask, ga_block, jnp.zeros_like(ga_block))
            scores = scores_of(q_block, k_ref[0:stop], begin, first, h)
            weights = jnp.exp(scores - jnp.max(scores, axis=-1, keepdims=True))
            probs = weights * (1.0 / jnp.sum(weights, axis=-1, keepdims=True))
            g_probs = nt(g_head, v_ref[0:stop])
            inner = jnp.sum(probs * g_probs, axis=-1, keepdims=True)
            g_scores = (probs * (g_probs - inner)).astype(BF16)
            dq = jnp.where(mask, nn(g_scores, k_ref[0:stop]), dq)
            many_q.append(jnp.where(mask, q_block, jnp.zeros_like(q_block)))
            many_g.append(g_head)
            many_p.append(probs.astype(BF16))
            many_s.append(g_scores)
        dk[0:stop] += tn(jnp.concatenate(many_s, axis=0), jnp.concatenate(many_q, axis=0))
        dv[0:stop] += tn(jnp.concatenate(many_p, axis=0), jnp.concatenate(many_g, axis=0))
        dq = turn(dq * SCALE, cos_ref[first:stop], sin_ref[first:stop], -1.0)
        gproj[first:stop, 0:256] = dq.astype(BF16)

    step_c(0)
    attention_back(0)
    attention_back(1)
    step_a(4)
    step_b(2)
    step_c(1)
    attention_back(2)
    attention_back(3)
    sum4.relay_near()
    step_a(5)

    def project_back(i, total):
        rows = pl.ds(pl.multiple_of(i * 128, 128), 128)
        d_key = turn(dk[rows], cos_ref[rows], sin_ref[rows], -1.0).astype(BF16)
        d_value = dv[rows].astype(BF16)
        gproj[rows, 256:512] = d_key
        gproj[rows, 512:768] = d_value
        row = [gproj[rows, 0:256].astype(F32), d_key.astype(F32), d_value.astype(F32)]
        return total + jnp.sum(jnp.concatenate(row, axis=1), axis=0, keepdims=True)

    bias = lax.fori_loop(0, 8, project_back, jnp.zeros((1, 768), F32))

    def normed_back(side):
        rows = [gproj[pl.ds(pl.multiple_of((2 * i + side) * 128, 128), 128)] for i in range(4)]
        rows = jnp.concatenate(rows, axis=0)
        for pair in range(8):
            weight = jnp.concatenate([wa[pair // 2, pair % 2, 0, 16:784], wa[pair // 2, pair % 2, 1, 16:784]], axis=1)
            part = nn(rows, weight).astype(BF16).reshape(4, 128, 256)
            parts[pl.ds(side * 4, 4), :, pair * 256 : (pair + 1) * 256] = part

    sum8 = ScatterTp(net, parts, got8, got8_half)
    normed_back(1 - net.zl)
    sum8.start_side()
    sum4.wait()
    load_middle.wait()
    out_ref[...] = (dtok_ref[...] + sum4.total()).astype(BF16)
    net.settle([sum4.half_p, sum4.half_m] + sum4.near_p + sum4.near_m)
    normed_back(net.zl)
    sum8.start_plane()
    step_b(3)
    step_c(2)
    for slot in range(8):
        chunk = slot % 4 * 2 + slot // 4
        flipped[0:256, slot * 128 : (slot + 1) * 128] = att_ref[chunk * 128 : (chunk + 1) * 128].T
    for pair in range(8):
        some = gb[:, :, pair * 256 : (pair + 1) * 256].reshape(1024, 256)
        product = nn(flipped[0:256], some).astype(BF16)
        wa[pair // 2, pair % 2, 0, 784:1040] = product[:, 0:128]
        wa[pair // 2, pair % 2, 1, 784:1040] = product[:, 128:256]
    net.settle([gather.zb_p, gather.zb_m, gather.fwd_p, gather.fwd_m, gather.za_p, gather.za_m, gather.fz_p, gather.fz_m])
    load_normed = net.move(normed_hbm, gb)
    sum8.relay_side()
    flipped[...] = gproj[...].T
    load_normed.wait()
    for pair in range(8):
        some = gb[:, :, pair * 256 : (pair + 1) * 256].reshape(1024, 256)
        product = nn(flipped[...], some).astype(BF16)
        wa[pair // 2, pair % 2, 0, 16:784] = product[:, 0:128]
        wa[pair // 2, pair % 2, 1, 16:784] = product[:, 128:256]
    first_core = net.send(wa.at[:, :, 1 - core, pl.ds(16, 1024)], theirs_a, "c")
    scatter_q = ScatterW(
        net, 1024, lambda yy: wa.at[yy, :, core, pl.ds(16, 1024)], lambda yy: theirs_a.at[yy], far_a, near_a
    )
    sum8.relay_across()
    step_b(4)
    step_c(3)
    first_core.wait_recv()
    scatter_q.step_a()
    sum8.relay_near()
    step_b(5)
    step_c(4)
    step_d(0)
    sum8.wait()
    given = sum8.total()
    grad, normed = norm_back(x_ref[...].astype(F32), given, gains[0:1])
    dtok_ref[...] = gmid_ref[...] + grad
    gain_sum = jnp.sum(given * normed, axis=0, keepdims=True)
    bias_sum = jnp.sum(given, axis=0, keepdims=True)
    bias_rows = jnp.concatenate([bias[:, i * 128 : (i + 1) * 128] for i in range(6)], axis=0)
    small_out[:, 4:10] = jnp.broadcast_to(bias_rows[None], (16, 6, 128))
    small_out[:, 10:16] = jnp.zeros((16, 6, 128), F32)
    for i in range(16):
        lanes = slice(i * 128, (i + 1) * 128)
        small_out[i, 0:1] = gain_sum[:, lanes]
        small_out[i, 1:2] = bias_sum[:, lanes]
        small_out[i, 2:4] = ln2_ref[0:2, lanes]
    copies = [
        net.send(small_out.at[place[0]], small_in.at[i], place) for i, place in enumerate(across_f)
    ]
    scatter_q.step_b()
    step_c(5)
    step_d(1)
    scatter_q.step_c()
    z_q = net.send(wa.at[y, 1 - zh, core, pl.ds(16, 1024)], by_z_a, "zh")
    step_d(2)
    total = small_out[f]
    for i, copy in enumerate(copies):
        copy.wait_recv()
        total = total + small_in[i]
    small_tp[...] = total
    copies = [net.send(small_tp.at[pl.ds(0, 8)], small_got.at[j], place) for j, place in enumerate(across_t)]
    z_q.wait_recv()

    da_ref[...] = wa[y, zh, core, pl.ds(16, 1024)].astype(F32) + by_z_a[...].astype(F32)
    row_id = lax.broadcasted_iota(jnp.int32, (8, 128), 0)
    total = small_tp[0:8]
    for j, copy in enumerate(copies):
        copy.wait_recv()
        total = total + jnp.where(row_id < 4, small_got[j], 0.0)
    small_ref[0:8] = total
    small_ref[8:16] = small_tp[8:16]
    net.finish()


def k3(x, lens, wa, gmid, middle, down, ln2, grads, normed, q, k, v, att):
    shapes = [
        ((128, 2048), BF16, VM), ((128, 2048), F32, VM), ((3, ROWS_M, 128), F32, VM), ((1024, 128), F32, VM),
        ((16, 128), F32, VM), ((6, 4, 2, ROWS_M, 128), BF16, AN),
    ]
    scratch = [
        ((1024, 256), BF16), ((1024, 256), BF16), ((1024, 256), BF16), ((1024, 256), BF16),
        ((4, 2, 2, ROWS_A, 128), BF16), ((8, 128, 2048), BF16), ((8, 128, 2048), BF16), ((3, 128, 2048), BF16),
        ((8, 64, 2048), BF16), ((2, 128, 2048), BF16), ((2, 64, 2048), BF16),
        ((128, 2048), BF16), ((8, 2048), F32), ((1024, 256), BF16), ((1024, 256), F32), ((1024, 256), F32),
        ((1024, 768), BF16), ((768, 1024), BF16), ((1024, 128), jnp.int32), ((1024, 128), F32), ((1024, 128), F32),
        ((6, 4, 2, ROWS_M, 128), BF16), ((2, 4, 2, ROWS_M, 128), BF16), ((6, 2, 2, ROWS_M // 2, 128), BF16),
        ((6, 2, 2, ROWS_M, 128), BF16), ((3, 3, ROWS_M, 128), BF16), ((4, 2, 1024, 128), BF16),
        ((2, 2, 512, 128), BF16), ((2, 2, 1024, 128), BF16),
        ((1024, 128), BF16), ((16, 16, 128), F32), ((15, 16, 128), F32), ((16, 128), F32), ((7, 8, 128), F32),
    ]
    return pl.pallas_call(
        k3_kernel,
        out_shape=[jax.ShapeDtypeStruct(s, d) for s, d, _ in shapes],
        in_specs=[VM, SM, AN, VM, AN, AN, VM, AN, AN, AN, AN, AN, AN],
        out_specs=[m for _, _, m in shapes],
        scratch_shapes=[pltpu.VMEM(s, d) for s, d in scratch]
        + [pltpu.SemaphoreType.DMA((160,)), pltpu.SemaphoreType.DMA((160,)), pltpu.SemaphoreType.DMA((24,))],
        compiler_params=pltpu.CompilerParams(
            collective_id=3, has_side_effects=True, vmem_limit_bytes=62 * MIB
        ),
        name="attend_back_sum_gradients",
    )(
        x, lens, wa.reshape(4, 2, 2, ROWS_A, 128), gmid, middle, down, ln2,
        grads.reshape(3, 2, 4, 2, 2, ROWS_M, 128), normed, q, k, v, att,
    )


def finish_kernel(
    out_in, dtok_in, dm_in, da_in, small_in,
    out_ref, dtok_ref, gain1, bias1, dqkv, dout, gain2, bias2, dgate, dup, ddown,
):
    out_ref[...] = out_in[...]
    dtok_ref[...] = dtok_in[...]
    for i, ref in enumerate((gain1, bias1, gain2, bias2)):
        ref[...] = small_in[i : i + 1]
    for j in range(3):
        for part in range(2):
            lanes = slice(part * 128, (part + 1) * 128)
            dqkv[j, :, lanes] = da_in[j * 256 + part * 128 : j * 256 + (part + 1) * 128].T
    dout[...] = da_in[768:1024]
    dgate[...] = dm_in[0]
    dup[...] = dm_in[1]
    ddown[...] = dm_in[2]


def finish(out, d_tokens, dm, da, small):
    shapes = [
        ((128, 2048), BF16), ((128, 2048), F32), ((1, 128), F32), ((1, 128), F32), ((3, 128, 256), F32), ((256, 128), F32),
        ((1, 128), F32), ((1, 128), F32), ((ROWS_M, 128), F32), ((ROWS_M, 128), F32), ((ROWS_M, 128), F32),
    ]
    return pl.pallas_call(
        finish_kernel,
        out_shape=[jax.ShapeDtypeStruct(s, d) for s, d in shapes],
        in_specs=[VM] * 5,
        out_specs=[VM] * 11,
        compiler_params=pltpu.CompilerParams(vmem_limit_bytes=62 * MIB),
        name="lay_out_gradients",
    )(out, d_tokens, dm, da, small)


def local(
    tokens, seq_lens, ln1_gain, ln1_bias, w_qkv, b_qkv, w_out, ln2_gain, ln2_bias, w_gate, w_up, w_down, cotangent
):
    small = small_rows(ln1_gain, ln1_bias, b_qkv, ln2_gain, ln2_bias)
    normed, wa, wg, cotg, q, k, v, att = k1(
        tokens, seq_lens, small, jnp.transpose(w_qkv, (1, 0, 2)), w_out, w_gate.T, cotangent
    )
    middle, gmid, down, grads, ln2 = k2(tokens, att, wa, wg, w_up.T, w_down, cotangent, cotg)
    out, d_tokens, dm, da, small, _ = k3(
        tokens, seq_lens, wa, gmid, middle, down, ln2, grads, normed, q, k, v, att
    )
    d_bias = lax.dynamic_slice_in_dim(
        small[4:10].reshape(3, 4, HEAD_DIM), lax.axis_index("fsdp") * 4, 4, axis=2
    )
    out, d_tokens, gain1, bias1, dqkv, dout, gain2, bias2, dgate, dup, ddown = finish(out, d_tokens, dm, da, small)
    return (
        out, d_tokens, gain1[0], bias1[0], jnp.transpose(dqkv, (1, 0, 2)), d_bias, dout, gain2[0], bias2[0], dgate.T, dup.T, ddown,
    )


def solution(mesh):
    placed = (
        P(("fsdp", "tp"), None),
        P("fsdp", None),
        P("fsdp"),
        P("fsdp"),
        P("fsdp", None, "tp"),
        P(None, "tp", "fsdp"),
        P("tp", "fsdp"),
        P("fsdp"),
        P("fsdp"),
        P("fsdp", "tp"),
        P("fsdp", "tp"),
        P("tp", "fsdp"),
        P(("fsdp", "tp"), None),
    )
    return jax.shard_map(
        local,
        mesh=mesh,
        in_specs=placed,
        out_specs=(
            P(("fsdp", "tp"), None),
            P(("fsdp", "tp"), None),
            P("fsdp"),
            P("fsdp"),
            P("fsdp", None, "tp"),
            P(None, "tp", "fsdp"),
            P("tp", "fsdp"),
            P("fsdp"),
            P("fsdp"),
            P("fsdp", "tp"),
            P("fsdp", "tp"),
            P("tp", "fsdp"),
        ),
        check_vma=False,
    )
```

time: 1540 us -> 320 us (0.21)
  waiting for transfers between devices: 1110 us -> 0 us
  Pallas kernels: 0 us -> 310 us
  blocking collectives: 203 us -> 0 us
  matrix products: 125 us -> 0 us
  other arithmetic: 42.8 us -> 1.39 us
  local copies, waits for them, and re-layouts: 35.7 us -> 2.32 us
  between operations: 16.8 us -> 0.88 us
    all_gather x9 -> x0, waiting for transfers between devices: 482 us -> none  [the longest x1 90.4 us: local(): normed_two_all = lax.all_gather(normed_two, 'tp', axis=0, tiled=True)]
    reduce_scatter x5 -> x0, waiting for transfers between devices: 384 us -> none  [the longest x1 91 us: local(): lax.psum_scatter(down_part.astype(jnp.bfloat16), 'tp', scatter_dimension=...]
    pallas_call x0 -> x4, Pallas kernels: none -> 310 us  [the longest x1 129 us: k3(): pl.pallas_call(k3_kernel, out_shape=[jax.ShapeDtypeStruct(s, d) for s, d,...]
    unnamed x22 -> x0, waiting for transfers between devices: 241 us -> none
    dot_general x25 -> x0, matrix products: 116 us -> none  [the longest x1 10.1 us: local(): jnp.einsum('td,fd->tf', grad_down, second_gather[9], preferred_element_ty...]
    all_gather x5 -> x0, blocking collectives: 115 us -> none  [the longest x1 25.5 us: local(): lax.all_gather(ln2_bias, 'fsdp', axis=0, tiled=True)]
    unnamed x1 -> x0, blocking collectives: 68.9 us -> none
    unnamed x127 -> x0, local copies, waits for them, and re-layouts: 32.1 us -> none
  transfers between devices with their start and end apart: 18 -> 0, of which waited for: 17 -> 0; matrix products, arithmetic and copies ran while one was open for 10% -> 0% of each run, Pallas kernels for 0% -> 0%
where the time goes in v1:
time: 320 us; the launch traced here: 315 us
  Pallas kernels  310 us (97%)
    pallas_call x1, Pallas kernels, k3(): pl.pallas_call(k3_kernel, out_shape=[jax.ShapeDtypeStruct(s, d) for s, d,...  129 us
    pallas_call x1, Pallas kernels, k2(): pl.pallas_call(k2_kernel, out_shape=[jax.ShapeDtypeStruct(s, d) for s, d,...  104 us
    pallas_call x1, Pallas kernels, k1(): pl.pallas_call(k1_kernel, out_shape=[hbm(s) for s in shapes], in_specs=[V...  73.5 us

profile of v1, /device:TPU:0, one launch (start us, length us, event | category | flops | bytes accessed | tf_op | source)
XLA Modules:
  0.0 314.6 jit_solution(18329073282022067690)
XLA Ops:
  0.7 0.7 copy.26
  1.4 0.1 dynamic_update_slice.3
  1.4 0.1 reshape.44
  1.6 1.4 select_select_fusion.small_ref
  2.9 73.5 %gather_project_attend.1 = (bf16[8,128,2048]{2,1,0:T(8,128)(2,1)}, bf16[16,1040,128]{2,1,0:T(8,128)(2,1)}, bf16[2,16,704,128]{3,2,1,0:T(8,128)(2,1)}, bf16[4,128...) custom-call(bf16[128,2048]{1,0:T(8,128)(2,1)} %x_ref.5, ...), custom_call_target="tpu_custom_call" | custom-call | tf_op jit(solution)/shard_map/gather_project_attend/pallas_call | solution.py:464
  76.5 103.6 %project_norm_feed_forward.1 = (f32[128,2048]{1,0:T(8,128)}, f32[128,2048]{1,0:T(8,128)}, bf16[4,128,2048]{2,1,0:T(8,128)(2,1)}, bf16[3,2,16,704,128]{4,3,2,1,0:T(8,128)(2,1)}, f32[8,2048]{1,0:T(8,128)}) custom-call(bf16[128,2048]{1,0:T(8,128)(2,1)} %x_ref.5, bf16[1024,256]{1,0:T(8,128)(2,1)} %get-tuple-element.42.att_ref.att_hbm, ...), custom_call_target="tpu_custom_call" | custom-call | tf_op jit(solution)/shard_map/project_norm_feed_forward/pallas_call | solution.py:800
  180.1 129.2 %attend_back_sum_gradients.1 = (bf16[128,2048]{1,0:T(8,128)(2,1)}, f32[128,2048]{1,0:T(8,128)}, f32[3,704,128]{2,1,0:T(8,128)}, f32[1024,128]{1,0:T(8,128)}, f32...) custom-call(bf16[128,2048]{1,0:T(8,128)(2,1)} %x_ref.5, s32[1,8]{1,0:T(1,128)} %lens_ref.3, ...), custom_call_target="tpu_custom_call" | custom-call | tf_op jit(solution)/shard_map/attend_back_sum_gradients/pallas_call | solution.py:1169
  309.3 3.7 %lay_out_gradients.1 = (bf16[128,2048]{1,0:T(8,128)(2,1)}, f32[128,2048]{1,0:T(8,128)}, f32[1,128]{1,0:T(1,128)}, f32[1,128]{1,0:T(1,128)}, f32[3,128,256]{2,1,0...) custom-call(bf16[128,2048]{1,0:T(8,128)(2,1)} %get-tuple-element.54., ...), custom_call_target="tpu_custom_call" | custom-call | tf_op jit(solution)/shard_map/lay_out_gradients/pallas_call | solution.py:1209
  313.0 0.7 slice.3
  313.7 0.1 reshape.47
  313.8 0.7 constant_dynamic-slice_fusion
  (3 shorter events, 0.0 us)
